TPU v7x, 32 devices: a whole 2x2x4 slice. The times are simulated.
32 devices in a mesh: wide: 8 (over y, x, core), narrow: 4 (over z).
Axes of the slice: x: 2, y: 2, z: 4, core: 2. Of those that a mesh axis runs over, the one named last changes fastest.
Arguments:
- inputs: bfloat16 [10240, 768], P(('wide', 'narrow')), may hold values from -6 to 6
- pass_ids: int32 [8, 1280], P('wide'), may hold values from 0 to 4, as said below
- front_gain: bfloat16 [768], replicated, may hold values from 0.25 to 1.75
- front_shift: bfloat16 [768], replicated, may hold values from -3 to 3
- triple_weight: bfloat16 [3, 768, 768], P(None, None, 'narrow'), may hold values from -0.21875 to 0.21875
- triple_bias: bfloat16 [2, 768], P(None, 'narrow'), may hold values from -3 to 3
- mixer_weight: bfloat16 [768, 768], replicated, may hold values from -0.875 to 0.875
- mixer_bias: bfloat16 [768], replicated, may hold values from -3 to 3
- back_gain: bfloat16 [768], replicated, may hold values from 0.25 to 1.75
- back_shift: bfloat16 [768], replicated, may hold values from -3 to 3
- expand_weight: bfloat16 [768, 3072], replicated, may hold values from -0.21875 to 0.21875
- expand_bias: bfloat16 [3072], replicated, may hold values from -3 to 3
- reduce_weight: bfloat16 [3072, 768], replicated, may hold values from -0.109375 to 0.109375
- reduce_bias: bfloat16 [768], replicated, may hold values from -3 to 3
- pass_table: bfloat16 [5, 768], replicated, may hold values from -3 to 3
- cotangent: bfloat16 [10240, 768], P(('wide', 'narrow')), may hold values from -15 to 15
Outputs:
- layer_out: bfloat16 [10240, 768], P(('wide', 'narrow'))
- grad_inputs: bfloat16 [10240, 768], P(('wide', 'narrow'))
- grad_front_gain: float32 [768], replicated
- grad_front_shift: float32 [768], replicated
- grad_triple_weight: float32 [3, 768, 768], P(None, None, 'narrow')
- grad_triple_bias: float32 [2, 768], P(None, 'narrow')
- grad_mixer_weight: float32 [768, 768], P('wide', 'narrow')
- grad_mixer_bias: float32 [768], replicated
- grad_back_gain: float32 [768], replicated
- grad_back_shift: float32 [768], replicated
- grad_expand_weight: float32 [768, 3072], P('wide', 'narrow')
- grad_expand_bias: float32 [3072], replicated
- grad_reduce_weight: float32 [3072, 768], P('wide', 'narrow')
- grad_reduce_bias: float32 [768], replicated
- grad_pass_table: float32 [5, 768], replicated
Inputs may be any that keep to these rules, and one draw needn't show every extreme that they name: `pass_ids`: in each sequence the first 5 rows are passes 0 to 4 of its first token; every later row has pass 0 or one more than the row before it.
All inputs are finite; a program needn't handle non-finite values.
Results may differ from a plain program's by a relative error of at most 0.013.
Values may be sent and summed in bfloat16 or wider, within the bound.
No kernel may reach another device: no remote copies, remote signals or barrier semaphores. Data moves between devices by JAX's collectives and lax.ppermute only.
A program may use at most 128 MiB of HBM per device.

v0:
```python
import jax
import jax.numpy as jnp
from jax import lax
from jax.sharding import PartitionSpec as P

HEAD_DIM = 64


epsilon = 1e-05


def for_sending(value):
    return jax.tree.map(lambda a: a.astype(jnp.bfloat16) if a.dtype == jnp.float32 else a, value)


def norm_forward(values, weight_gain, weight_shift):
    row_mean = jnp.mean(values, axis=-1, keepdims=True)
    centred = values - row_mean
    inv_scale = lax.rsqrt(jnp.mean(centred * centred, axis=-1, keepdims=True) + epsilon)
    unit_rows = centred * inv_scale
    return (unit_rows * weight_gain + weight_shift, unit_rows, inv_scale)


def norm_backward(grad_out, unit_rows, inv_scale, weight_gain):
    grad_unit = grad_out * weight_gain
    inner_sum = (
        grad_unit
        - jnp.mean(grad_unit, axis=-1, keepdims=True)
        - unit_rows * jnp.mean(grad_unit * unit_rows, axis=-1, keepdims=True)
    )
    return (inner_sum * inv_scale, jnp.sum(grad_out * unit_rows, axis=0), jnp.sum(grad_out, axis=0))


def visible_pairs(seq_ids):
    positions = jnp.cumsum((seq_ids == 0).astype(jnp.int32)) - 1
    return (positions[None, :] <= positions[:, None]) & (seq_ids[None, :] <= seq_ids[:, None])


def block_size():
    return 640


def masked_scores(query_block, key_rows, visible, first_row, block_rows):
    factor = query_block.shape[-1] ** (-0.5)
    scores = (
        jnp.einsum("qhe,khe->hqk", query_block, key_rows, preferred_element_type=jnp.float32)
        * factor
    )
    return jnp.where(visible[None, first_row : first_row + block_rows], scores, -1e30)


def attend_forward(arrays):
    queries, key_rows, value_rows, seq_ids = arrays
    visible = visible_pairs(seq_ids)
    row_count = queries.shape[0]
    block_rows = block_size()
    outputs = []
    log_totals = []
    for first_row in range(0, row_count, block_rows):
        query_block = queries[first_row : first_row + block_rows]
        scores = masked_scores(query_block, key_rows, visible, first_row, block_rows)
        row_top = jnp.max(scores, axis=-1, keepdims=True)
        exp_scores = jnp.exp(scores - row_top)
        row_total = jnp.sum(exp_scores, axis=-1, keepdims=True)
        probs = (exp_scores / row_total).astype(jnp.bfloat16)
        outputs.append(
            jnp.einsum(
                "hqk,khe->qhe", probs, value_rows, preferred_element_type=jnp.float32
            ).astype(jnp.bfloat16)
        )
        log_totals.append((row_top + jnp.log(row_total))[..., 0])
    return (jnp.concatenate(outputs, axis=0), jnp.concatenate(log_totals, axis=1))


def attend_backward(arrays):
    queries, key_rows, value_rows, seq_ids, log_totals, grad_rows = arrays
    visible = visible_pairs(seq_ids)
    row_count = queries.shape[0]
    block_rows = block_size()
    factor = queries.shape[-1] ** (-0.5)
    grad_queries = []
    grad_keys = jnp.zeros(key_rows.shape, jnp.float32)
    grad_values = jnp.zeros(value_rows.shape, jnp.float32)
    for first_row in range(0, row_count, block_rows):
        query_block = queries[first_row : first_row + block_rows]
        grad_block = grad_rows[first_row : first_row + block_rows]
        scores = masked_scores(query_block, key_rows, visible, first_row, block_rows)
        probs = jnp.exp(scores - log_totals[:, first_row : first_row + block_rows, None])
        grad_probs = jnp.einsum(
            "qhe,khe->hqk", grad_block, value_rows, preferred_element_type=jnp.float32
        )
        inner_sum = jnp.sum(probs * grad_probs, axis=-1, keepdims=True)
        grad_scores = (probs * (grad_probs - inner_sum)).astype(jnp.bfloat16)
        grad_queries.append(
            jnp.einsum("hqk,khe->qhe", grad_scores, key_rows, preferred_element_type=jnp.float32)
            * factor
        )
        grad_keys = (
            grad_keys
            + jnp.einsum(
                "hqk,qhe->khe", grad_scores, query_block, preferred_element_type=jnp.float32
            )
            * factor
        )
        grad_values = grad_values + jnp.einsum(
            "hqk,qhe->khe",
            probs.astype(jnp.bfloat16),
            grad_block,
            preferred_element_type=jnp.float32,
        )
    return (
        jnp.concatenate(grad_queries, axis=0).astype(jnp.bfloat16),
        grad_keys.astype(jnp.bfloat16),
        grad_values.astype(jnp.bfloat16),
    )


def with_key_zero(bias_pair):
    return jnp.stack([bias_pair[0], jnp.zeros_like(bias_pair[0]), bias_pair[1]]).astype(jnp.float32)


def body(
    inputs,
    pass_ids,
    front_gain,
    front_shift,
    triple_weight,
    triple_bias,
    mixer_weight,
    mixer_bias,
    back_gain,
    back_shift,
    expand_weight,
    expand_bias,
    reduce_weight,
    reduce_bias,
    pass_table,
    cotangent,
):
    local_rows, width = inputs.shape
    seq_count, seq_rows = pass_ids.shape
    head_size = HEAD_DIM
    heads_here = triple_weight.shape[2] // head_size
    start_row = lax.axis_index("narrow") * local_rows
    own_ids = lax.dynamic_slice_in_dim(pass_ids.reshape(-1), start_row, local_rows)
    one_hot = (
        own_ids[:, None] == jnp.arange(pass_table.shape[0], dtype=jnp.int32)[None, :]
    ).astype(jnp.float32)
    x_rows = inputs.astype(jnp.float32)
    front_gain_f = front_gain.astype(jnp.float32)
    back_gain_f = back_gain.astype(jnp.float32)
    normed, unit_one, scale_one = norm_forward(
        x_rows, front_gain_f, front_shift.astype(jnp.float32)
    )
    normed_low = normed.astype(jnp.bfloat16)
    full_weight, full_bias = (
        lax.all_gather(triple_weight, "narrow", axis=2, tiled=True),
        lax.all_gather(triple_bias, "narrow", axis=1, tiled=True),
    )
    projected = jnp.einsum(
        "md,sde->sme", normed_low, full_weight, preferred_element_type=jnp.float32
    )
    triple_rows = (projected + with_key_zero(full_bias)[:, None, :]).astype(jnp.bfloat16)
    triple_heads = lax.all_to_all(triple_rows, "narrow", split_axis=2, concat_axis=1, tiled=True)
    shaped = triple_heads.reshape(3, seq_count, seq_rows, heads_here, head_size)
    attended, log_totals = lax.map(attend_forward, (shaped[0], shaped[1], shaped[2], pass_ids))
    mixed_heads = attended.reshape(seq_count * seq_rows, heads_here * head_size)
    mixed_rows = lax.all_to_all(
        for_sending(mixed_heads), "narrow", split_axis=0, concat_axis=1, tiled=True
    ).astype(mixed_heads.dtype)
    branch = jnp.dot(
        mixed_rows, mixer_weight, preferred_element_type=jnp.float32
    ) + mixer_bias.astype(jnp.float32)
    middle = x_rows + branch
    normed_two, unit_two, scale_two = norm_forward(
        middle, back_gain_f, back_shift.astype(jnp.float32)
    )
    normed_two_low = normed_two.astype(jnp.bfloat16)
    hidden = jnp.dot(
        normed_two_low, expand_weight, preferred_element_type=jnp.float32
    ) + expand_bias.astype(jnp.float32)
    active_low = jax.nn.gelu(hidden).astype(jnp.bfloat16)
    second = jnp.dot(
        active_low, reduce_weight, preferred_element_type=jnp.float32
    ) + reduce_bias.astype(jnp.float32)
    embedded = jnp.dot(
        one_hot,
        pass_table.astype(jnp.float32),
        precision=lax.Precision.HIGHEST,
        preferred_element_type=jnp.float32,
    )
    layer_out = (middle + second + embedded).astype(jnp.bfloat16)
    grad_rows = cotangent.astype(jnp.float32)
    grad_table = jnp.dot(
        one_hot.T, grad_rows, precision=lax.Precision.HIGHEST, preferred_element_type=jnp.float32
    )
    grad_reduce_bias = jnp.sum(grad_rows, axis=0)
    grad_reduce = jnp.dot(active_low.T, cotangent, preferred_element_type=jnp.float32)
    grad_active = jnp.dot(cotangent, reduce_weight.T, preferred_element_type=jnp.float32)
    _, gelu_pull = jax.vjp(jax.nn.gelu, hidden)
    grad_hidden_low = gelu_pull(grad_active)[0].astype(jnp.bfloat16)
    grad_expand_bias = jnp.sum(grad_hidden_low.astype(jnp.float32), axis=0)
    grad_expand = jnp.dot(normed_two_low.T, grad_hidden_low, preferred_element_type=jnp.float32)
    grad_normed_two = jnp.dot(grad_hidden_low, expand_weight.T, preferred_element_type=jnp.float32)
    back_rows, grad_back_gain, grad_back_shift = norm_backward(
        grad_normed_two, unit_two, scale_two, back_gain_f
    )
    grad_middle = grad_rows + back_rows
    grad_middle_low = grad_middle.astype(jnp.bfloat16)
    grad_mixer_bias = jnp.sum(grad_middle_low.astype(jnp.float32), axis=0)
    grad_mixer = jnp.dot(mixed_rows.T, grad_middle_low, preferred_element_type=jnp.float32)
    grad_mixed_low = jnp.dot(
        grad_middle_low, mixer_weight.T, preferred_element_type=jnp.float32
    ).astype(jnp.bfloat16)
    grad_heads = lax.all_to_all(grad_mixed_low, "narrow", split_axis=1, concat_axis=0, tiled=True)
    grad_shaped = grad_heads.reshape(seq_count, seq_rows, heads_here, head_size)
    grad_q, grad_k, grad_v = lax.map(
        attend_backward, (shaped[0], shaped[1], shaped[2], pass_ids, log_totals, grad_shaped)
    )
    grad_triple_heads = jnp.stack([grad_q, grad_k, grad_v]).reshape(
        3, seq_count * seq_rows, heads_here * head_size
    )
    grad_triple_rows = lax.all_to_all(
        for_sending(grad_triple_heads), "narrow", split_axis=1, concat_axis=2, tiled=True
    ).astype(grad_triple_heads.dtype)
    term_weight = jnp.einsum(
        "md,sme->sde", normed_low, grad_triple_rows, preferred_element_type=jnp.float32
    )
    row_sums = jnp.sum(grad_triple_rows.astype(jnp.float32), axis=1)
    term_bias = jnp.stack([row_sums[0], row_sums[2]])
    grad_triple, grad_triple_bias = (
        lax.psum_scatter(
            term_weight.astype(jnp.bfloat16), "narrow", scatter_dimension=2, tiled=True
        ).astype(jnp.float32),
        lax.psum_scatter(
            term_bias.astype(jnp.bfloat16), "narrow", scatter_dimension=1, tiled=True
        ).astype(jnp.float32),
    )
    grad_normed = jnp.einsum(
        "sme,sde->md", grad_triple_rows, full_weight, preferred_element_type=jnp.float32
    )
    front_rows, grad_front_gain, grad_front_shift = norm_backward(
        grad_normed, unit_one, scale_one, front_gain_f
    )
    grad_inputs = (grad_middle + front_rows).astype(jnp.bfloat16)
    grad_triple, grad_triple_bias = lax.psum((grad_triple, grad_triple_bias), "wide")
    group_mixer, group_expand, group_reduce = (
        lax.psum_scatter(
            grad_mixer.astype(jnp.bfloat16), "narrow", scatter_dimension=1, tiled=True
        ).astype(jnp.float32),
        lax.psum_scatter(
            grad_expand.astype(jnp.bfloat16), "narrow", scatter_dimension=1, tiled=True
        ).astype(jnp.float32),
        lax.psum_scatter(
            grad_reduce.astype(jnp.bfloat16), "narrow", scatter_dimension=1, tiled=True
        ).astype(jnp.float32),
    )
    total_mixer, total_expand, total_reduce = (
        lax.psum_scatter(group_mixer, "wide", scatter_dimension=0, tiled=True),
        lax.psum_scatter(group_expand, "wide", scatter_dimension=0, tiled=True),
        lax.psum_scatter(group_reduce, "wide", scatter_dimension=0, tiled=True),
    )
    small_sums = lax.psum(
        (
            grad_front_gain,
            grad_front_shift,
            grad_mixer_bias,
            grad_back_gain,
            grad_back_shift,
            grad_expand_bias,
            grad_reduce_bias,
            grad_table,
        ),
        ("wide", "narrow"),
    )
    return (
        layer_out,
        grad_inputs,
        small_sums[0],
        small_sums[1],
        grad_triple,
        grad_triple_bias,
        total_mixer,
        small_sums[2],
        small_sums[3],
        small_sums[4],
        total_expand,
        small_sums[5],
        total_reduce,
        small_sums[6],
        small_sums[7],
    )


def solution(mesh):
    return jax.shard_map(
        body,
        mesh=mesh,
        in_specs=(
            P(("wide", "narrow"), None),
            P("wide", None),
            P(),
            P(),
            P(None, None, "narrow"),
            P(None, "narrow"),
            P(),
            P(),
            P(),
            P(),
            P(),
            P(),
            P(),
            P(),
            P(),
            P(("wide", "narrow"), None),
        ),
        out_specs=(
            P(("wide", "narrow"), None),
            P(("wide", "narrow"), None),
            P(),
            P(),
            P(None, None, "narrow"),
            P(None, "narrow"),
            P("wide", "narrow"),
            P(),
            P(),
            P(),
            P("wide", "narrow"),
            P(),
            P("wide", "narrow"),
            P(),
            P(),
        ),
        check_vma=False,
    )
```

profile of v0, /device:TPU:3, one launch (start us, length us, event | category | flops | bytes accessed | tf_op | source)
XLA Modules:
  0.0 699.5 jit_solution(3660519016239465478)
XLA Ops:
  9.3 9.4 %all-gather = bf16[4,192,2]{1,2,0:T(2,128)(2,1)S(1)} all-gather(bf16[1,192,2]{1,2,0:T(2,128)(2,1)} %bitcast.122), channel_id=1, replica_groups=mesh['wide'=8,'narrow'=4] {'narrow'}, dimensions={0}, use_global_device_ids=true | all-gather | bytes 3840 | tf_op jit(solution)/shard_map/all_gather | solution.py:158
  21.6 59.2 %all-gather.3.cloned.1.call-done = bf16[3,768,768]{1,2,0:T(8,128)(2,1)} async-done(((bf16[3,768,192]{1,2,0:T(8,128)(2,1)}), bf16[3,768,768]{1,2,0:T(8,128)(2,1)}) %all-gather.3.cloned.1.call-update) | async-done | bytes 3538960 | tf_op jit(solution)/shard_map/all_gather | solution.py:157
  99.4 45.4 %all-to-all-done = bf16[3,320,768]{1,0,2:T(4,128)(2,1)S(1)} async-done(((bf16[3,320,768]{1,0,2:T(4,128)(2,1)}), bf16[3,320,768]{1,0,2:T(4,128)(2,1)S(1)}, u32[]{:S(2)}, u32[]{:S(2)}) %all-to-all-start) | async-done | bytes 1474592 | tf_op jit(solution)/shard_map/all_to_all | solution.py:164
  179.7 6.2 fusion.70
  185.9 9.1 %all-to-all-done.1 = bf16[4,320,192]{1,2,0:T(8,128)(2,1)} async-done(((bf16[4,320,192]{1,2,0:T(8,128)(2,1)}), bf16[4,320,192]{1,2,0:T(8,128)(2,1)}, u32[]{:S(2)}, u32[]{:S(2)}) %all-to-all-start.1) | async-done | bytes 491552 | tf_op jit(solution)/shard_map/all_to_all | solution.py:168
  197.3 9.0 %convert_reduce_fusion = (f32[3072]{0:T(1024)S(1)}, bf16[320,3072]{1,0:T(8,128)(2,1)S(1)}, f32[320,3072]{1,0:T(8,128)}) fusion(f32[320,3072]{1,0:T(8,128)S(1)} %copy-done.35, f32[3072]{0:T(1024)S(1)} %convert_element_type.198, bf16[768,3072]{1,0:T(8,128)(2,1)} %param.26, f32[320,768]{1,0:T(8,128)S(1)} %get-tuple-element.198, ...), kind=kOutput, calls=%fused_computation.35 | convolution fusion | flops 1533785088 | bytes 15565312 | tf_op jit(solution)/shard_map/dot_general | solution.py:179
  211.9 7.2 %convolution_convert_fusion = bf16[3072,768]{0,1:T(8,128)(2,1)} fusion(bf16[320,768]{1,0:T(8,128)(2,1)} %param.31, f32[320,3072]{1,0:T(8,128)} %get-tuple-element.199), kind=kOutput, calls=%fused_computation.19 | convolution fusion | flops 1521156096 | bytes 9142272 | tf_op jit(solution)/shard_map/dot_general | solution.py:198
  226.1 6.8 convolution_convert_fusion.1
  233.2 19.2 %all-to-all-done.2 = bf16[320,4,192]{0,2,1:T(8,128)(2,1)S(1)} async-done(((bf16[320,4,192]{0,2,1:T(8,128)(2,1)}), bf16[320,4,192]{0,2,1:T(8,128)(2,1)S(1)}, u32[]{:S(2)}, u32[]{:S(2)}) %all-to-all-start.2) | async-done | bytes 491552 | tf_op jit(solution)/shard_map/all_to_all | solution.py:215
  254.9 5.8 fusion.4
  260.8 6.2 fusion.23
  270.7 5.9 multiply_reduce_fusion.1
  276.7 5.6 multiply_convert_fusion.1
  301.8 6.1 pad_maximum_fusion
  307.9 126.9 %all_to_all.68 = bf16[3,1280,192]{2,0,1:T(4,128)(2,1)} all-to-all(bf16[3,1280,192]{2,0,1:T(4,128)(2,1)S(1)} %pad_maximum_fusion), channel_id=1, replica_groups=mesh['wide'=8,'narrow'=4] {'narrow'}, dimensions={1} | all-to-all | bytes 2949120 | tf_op jit(solution)/shard_map/all_to_all | solution.py:223
  438.9 5.4 copy.123
  444.6 5.4 convert_bitcast_fusion
  455.3 7.2 %reduce-scatter.17.cloned.1.call-done = bf16[768,768]{1,0:T(8,128)(2,1)} async-done(((bf16[768,3072]{1,0:T(8,128)(2,1)}), bf16[768,768]{1,0:T(8,128)(2,1)}) %reduce-scatter.17.cloned.1.call-update) | async-done | bytes 1179664 | tf_op jit(solution)/shard_map/reduce_scatter | solution.py:251
  466.5 6.1 fusion.28
  476.2 48.6 %all-reduce = (f32[768]{0:T(1024)}, f32[768]{0:T(1024)}, f32[768]{0:T(1024)}, f32[768]{0:T(1024)}, f32[768]{0:T(1024)}, /*index=5*/f32[3072]{0:T(1024)}, f32[768]{0:T(1024)}, f32[5,768]{1,0:T(8,128)}) all-reduce(f32[768]{0:T(1024)S(1)} %get-tuple-element.158, ...), channel_id=1, replica_groups=mesh['wide'=8,'narrow'=4] {'wide','narrow'}, use_global_device_ids=true, to_apply=%region_17.18 | all-reduce | flops 11520 | bytes 92160 | tf_op jit(solution)/shard_map/psum | solution.py:263
  528.1 29.3 %reduce-scatter.13.cloned.1.call-done = bf16[3,768,192]{1,2,0:T(8,128)(2,1)} async-done(((bf16[3,768,768]{1,2,0:T(8,128)(2,1)}), bf16[3,768,192]{1,2,0:T(8,128)(2,1)}) %reduce-scatter.13.cloned.1.call-update) | async-done | bytes 884752 | tf_op jit(solution)/shard_map/reduce_scatter | solution.py:232
  557.4 57.5 %all-reduce.3 = (f32[3,768,192]{1,2,0:T(8,128)}, f32[2,192]{1,0:T(2,128)}) all-reduce(bf16[3,768,192]{1,2,0:T(8,128)(2,1)} %reduce-scatter.13.cloned.1.call-done, bf16[2,192]{1,0:T(2,128)(2,1)S(1)} %copy.135), channel_id=1, replica_groups=mesh['wide'=8,'narrow'=4] {'wide'}, use_global_device_ids=true, to_apply=%region_21.22 | all-reduce | flops 442752 | bytes 2656512 | tf_op jit(solution)/shard_map/psum | solution.py:246
  614.9 31.2 %reduce-scatter.23.cloned.1.call-done = f32[384,192]{0,1:T(8,128)} async-done(((f32[3072,192]{0,1:T(8,128)}), f32[384,192]{0,1:T(8,128)}) %reduce-scatter.23.cloned.1.call-update) | async-done | bytes 294928 | tf_op jit(solution)/shard_map/reduce_scatter | solution.py:261
  646.1 46.5 %reduce-scatter.19.cloned.1.call-done = f32[96,768]{1,0:T(8,128)} async-done(((f32[768,768]{1,0:T(8,128)}), f32[96,768]{1,0:T(8,128)}) %reduce-scatter.19.cloned.1.call-update) | async-done | bytes 294928 | tf_op jit(solution)/shard_map/reduce_scatter | solution.py:260
  (203 shorter events, 119.2 us)
Async XLA Ops:
  7.2 187.8 %copy-start = (bf16[768,768]{1,0:T(8,128)(2,1)S(1)}, bf16[768,768]{1,0:T(8,128)(2,1)}, u32[]{:S(2)}) copy-start(bf16[768,768]{1,0:T(8,128)(2,1)} %param.22) | copy-start | bytes 3538948
  7.2 73.6 %all-gather.3.cloned.1.call-start = ((), (), s32[]{:S(2)}) async-start(), calls=%async_computation.12 | async-start | bytes 4423680 | tf_op jit(solution)/shard_map/all_gather | solution.py:157
  8.6 75.8 %copy-start.21 = (f32[768]{0:T(1024)}, f32[768]{0:T(1024)S(1)}, u32[]{:S(2)}) copy-start(f32[768]{0:T(1024)S(1)} %convert_element_type.180) | copy-start | bytes 9220
  9.3 75.1 %copy-start.28 = (f32[768]{0:T(1024)}, f32[768]{0:T(1024)S(1)}, u32[]{:S(2)}) copy-start(f32[768]{0:T(1024)S(1)} %convert_element_type.181) | copy-start | bytes 9220
  20.1 64.3 %copy-start.19 = (f32[320]{0:T(512)}, f32[320]{0:T(512)S(1)}, u32[]{:S(2)}) copy-start(f32[320]{0:T(512)S(1)} %broadcast_multiply_fusion.5) | copy-start | bytes 3844
  21.5 63.0 %copy-start.25 = (f32[320]{0:T(512)}, f32[320]{0:T(512)S(1)}, u32[]{:S(2)}) copy-start(f32[320]{0:T(512)S(1)} %add_rsqrt_fusion.1) | copy-start | bytes 3844
  87.8 57.0 %all-to-all-start = ((bf16[3,320,768]{1,0,2:T(4,128)(2,1)}), bf16[3,320,768]{1,0,2:T(4,128)(2,1)S(1)}, u32[]{:S(2)}, u32[]{:S(2)}) async-start(bf16[3,320,768]{1,0,2:T(4,128)(2,1)} %copy.109), calls=%async_computation | async-start | bytes 4718592 | tf_op jit(solution)/shard_map/all_to_all | solution.py:164
  175.4 19.6 %all-to-all-start.1 = ((bf16[4,320,192]{1,2,0:T(8,128)(2,1)}), bf16[4,320,192]{1,2,0:T(8,128)(2,1)}, u32[]{:S(2)}, u32[]{:S(2)}) async-start(bf16[4,320,192]{1,2,0:T(8,128)(2,1)} %copy.115), calls=%async_computation.1 | async-start | bytes 1179648 | tf_op jit(solution)/shard_map/all_to_all | solution.py:168
  179.6 270.5 %reduce-scatter.15.cloned.1.call-start = ((), (), s32[]{:S(2)}) async-start(), calls=%async_computation.14 | async-start | bytes 1474560 | tf_op jit(solution)/shard_map/reduce_scatter | solution.py:248
  179.7 15.3 %copy-start.7 = (bf16[320,768]{1,0:T(8,128)(2,1)S(1)}, bf16[320,768]{1,0:T(8,128)(2,1)}, u32[]{:S(2)}) copy-start(bf16[320,768]{1,0:T(8,128)(2,1)} %param.16) | copy-start | bytes 1474564
  195.0 11.3 %slice-start.3 = ((s8[4718592]{0:T(1024)(128)(4,1)}), s8[4194304]{0:T(1024)(128)(4,1)S(1)}, s32[]{:S(2)}) async-start(s8[4718592]{0:T(1024)(128)(4,1)} %bitcast.123), calls=%async_computation.24 | async-start | bytes 8388608
  196.9 11.5 %copy-start.9 = (f32[320,768]{1,0:T(8,128)}, f32[320,768]{1,0:T(8,128)S(1)}, u32[]{:S(2)}) copy-start(f32[320,768]{1,0:T(8,128)S(1)} %get-tuple-element.198) | copy-start | bytes 2949124
  211.8 240.4 %reduce-scatter.21.cloned.1.call-start = ((), (), s32[]{:S(2)}) async-start(), calls=%async_computation.17 | async-start | bytes 5898240 | tf_op jit(solution)/shard_map/reduce_scatter | solution.py:254
  222.5 29.9 %all-to-all-start.2 = ((bf16[320,4,192]{0,2,1:T(8,128)(2,1)}), bf16[320,4,192]{0,2,1:T(8,128)(2,1)S(1)}, u32[]{:S(2)}, u32[]{:S(2)}) async-start(bf16[320,4,192]{0,2,1:T(8,128)(2,1)} %bitcast.13), calls=%async_computation.2 | async-start | bytes 1179648 | tf_op jit(solution)/shard_map/all_to_all | solution.py:215
  226.0 236.5 %reduce-scatter.17.cloned.1.call-start = ((), (), s32[]{:S(2)}) async-start(), calls=%async_computation.15 | async-start | bytes 5898240 | tf_op jit(solution)/shard_map/reduce_scatter | solution.py:251
  233.0 294.2 %reduce-scatter.25.cloned.1.call-start = ((), (), s32[]{:S(2)}) async-start(), calls=%async_computation.19 | async-start | bytes 245760
  270.7 12.4 %slice-start = ((s8[9830400]{0:T(1024)(128)(4,1)}), s8[4194304]{0:T(1024)(128)(4,1)S(1)}, s32[]{:S(2)}) async-start(s8[9830400]{0:T(1024)(128)(4,1)} %bitcast.105), calls=%async_computation.21 | async-start | bytes 8388608
  270.7 12.4 %slice-start.1 = ((s8[9830400]{0:T(1024)(128)(4,1)}), s8[4194304]{0:T(1024)(128)(4,1)S(1)}, s32[]{:S(2)}) async-start(s8[9830400]{0:T(1024)(128)(4,1)} %bitcast.105), calls=%async_computation.22 | async-start | bytes 8388608
  444.3 113.1 %reduce-scatter.13.cloned.1.call-start = ((), (), s32[]{:S(2)}) async-start(), calls=%async_computation.13 | async-start | bytes 4423680 | tf_op jit(solution)/shard_map/reduce_scatter | solution.py:232
  450.0 164.9 %reduce-scatter.27.cloned.1.call-start = ((), (), s32[]{:S(2)}) async-start(), calls=%async_computation.20 | async-start | bytes 884736
  452.1 194.0 %reduce-scatter.23.cloned.1.call-start = ((), (), s32[]{:S(2)}) async-start(), calls=%async_computation.18 | async-start | bytes 2654208 | tf_op jit(solution)/shard_map/reduce_scatter | solution.py:261
  455.2 11.3 %copy-start.10 = (f32[320,768]{1,0:T(8,128)S(1)}, f32[320,768]{1,0:T(8,128)}, u32[]{:S(2)}) copy-start(f32[320,768]{1,0:T(8,128)} %copy-done.9) | copy-start | bytes 2949124
  455.3 237.3 %reduce-scatter.19.cloned.1.call-start = ((), (), s32[]{:S(2)}) async-start(), calls=%async_computation.16 | async-start | bytes 2654208 | tf_op jit(solution)/shard_map/reduce_scatter | solution.py:260
  472.6 220.0 %copy-start.1 = (bf16[768,768]{1,0:T(8,128)(2,1)S(1)}, bf16[768,768]{1,0:T(8,128)(2,1)}, u32[]{:S(2)}) copy-start(bf16[768,768]{1,0:T(8,128)(2,1)} %param.22) | copy-start | bytes 3538948
  (30 other events, 190.9 us)
Sparse Core Ops, SparseCore 0:
  9.6 71.1 all-gather.2
  212.0 37.1 reduce-scatter.14
  251.5 106.9 reduce-scatter.20
  360.7 101.8 reduce-scatter.16
  464.6 22.9 reduce-scatter.24
  489.9 67.3 reduce-scatter.12
  561.4 37.3 reduce-scatter.26
  603.1 43.0 reduce-scatter.22
  650.1 42.4 reduce-scatter.18
where the time goes:
time: 711 us; the launch traced here: 700 us
  waiting for transfers between devices  248 us (35%)
  blocking collectives  242 us (34%)
  matrix products  94.6 us (13%)
  local copies, waits for them, and re-layouts  48.9 us (7%)
  other arithmetic  38.5 us (5%)
  between operations  15 us (2%)
  starting transfers between devices  12 us (2%)
    all_to_all x1, blocking collectives, body(): lax.all_to_all(for_sending(grad_triple_heads), 'narrow', split_axis=1, co...  127 us
    all_gather x1, waiting for transfers between devices, body(): lax.all_gather(triple_weight, 'narrow', axis=2, tiled=True)  59.2 us
    psum x1, blocking collectives, body(): lax.psum((grad_triple, grad_triple_bias), 'wide')  57.5 us
    psum x1, blocking collectives, body(): lax.psum((grad_front_gain, grad_front_shift, grad_mixer_bias, grad_back_g...  48.6 us
    reduce_scatter x1, waiting for transfers between devices, body(): lax.psum_scatter(group_expand, 'wide', scatter_dimension=0, tiled=True)  46.5 us
    all_to_all x1, waiting for transfers between devices, body(): lax.all_to_all(triple_rows, 'narrow', split_axis=2, concat_axis=1, tiled=...  45.4 us
    reduce_scatter x1, waiting for transfers between devices, body(): lax.psum_scatter(group_reduce, 'wide', scatter_dimension=0, tiled=True)  31.2 us
    reduce_scatter x1, waiting for transfers between devices, body(): lax.psum_scatter(term_weight.astype(jnp.bfloat16), 'narrow', scatter_dime...  29.3 us
  transfers between devices with their start and end apart: 12, of which 8 were waited for; matrix products, arithmetic and copies ran while one was open for 18% of the time, Pallas kernels for 0%

commit v1 on v0

v1 whole, which is shorter than its diff:
```python
import functools
import math

import jax
import jax.numpy as jnp
from jax import lax
from jax.experimental import pallas as pl
from jax.experimental.pallas import tpu as pltpu
from jax.sharding import PartitionSpec as P

HEAD_DIM = 64
EPSILON = 1e-05
BLOCK = 256
HIDDEN = -1e30
F32 = jnp.float32
BF16 = jnp.bfloat16
VMEM_LIMIT = 60 * 1024 * 1024
NN = (((1,), (0,)), ((), ()))
NT = (((1,), (1,)), ((), ()))
TN = (((0,), (0,)), ((), ()))
GELU_A = math.sqrt(2.0 / math.pi)
GELU_B = 0.044715


def dot(left, right, dims=NN):
    return lax.dot_general(left, right, dims, preferred_element_type=F32)


def whole():
    return pl.BlockSpec(memory_space=pltpu.VMEM)


def params(**more):
    return pltpu.CompilerParams(vmem_limit_bytes=VMEM_LIMIT, **more)


def unit_rows(values):
    centred = values - jnp.mean(values, axis=-1, keepdims=True)
    scale = lax.rsqrt(jnp.mean(centred * centred, axis=-1, keepdims=True) + EPSILON)
    return centred * scale, scale


def norm_pullback(grad_out, unit, scale, gain):
    grad_unit = grad_out * gain
    inner = (
        grad_unit
        - jnp.mean(grad_unit, axis=-1, keepdims=True)
        - unit * jnp.mean(grad_unit * unit, axis=-1, keepdims=True)
    )
    return inner * scale


def keep_head(block, head, axis):
    place = lax.broadcasted_iota(jnp.int32, block.shape, axis) // HEAD_DIM
    return jnp.where(place == head, block, jnp.zeros_like(block))


def visibility(ids_col_ref, ids_row_ref, start, keys):
    seen = ids_col_ref[0:keys, :] <= ids_row_ref[:, start : start + BLOCK]
    key_place = lax.broadcasted_iota(jnp.int32, (keys, BLOCK), 0)
    query_place = lax.broadcasted_iota(jnp.int32, (keys, BLOCK), 1) + start
    return jnp.where(seen & (key_place <= query_place), 0.0, HIDDEN).astype(F32)


def attend_forward_kernel(
    x_ref, ids_row_ref, ids_col_ref, gain_ref, shift_ref, weight_ref, bias_ref,
    mixed_ref, mixed_t_ref, lse_ref, normed_ref, q_ref, k_ref, v_ref, q_t_ref, k_t_ref,
    v_t_ref, bias_t_ref,
):
    rows = x_ref.shape[0]
    heads = weight_ref.shape[2] // HEAD_DIM
    gain = gain_ref[...].astype(F32)
    shift = shift_ref[...].astype(F32)

    def project(step, carry):
        here = pl.ds(pl.multiple_of(step * BLOCK, BLOCK), BLOCK)
        unit, _ = unit_rows(x_ref[here, :].astype(F32))
        normed = (unit * gain + shift).astype(BF16)
        normed_ref[here, :] = normed
        q = (dot(normed, weight_ref[0]) + bias_ref[0:1, :].astype(F32)).astype(BF16)
        q = q * jnp.asarray(HEAD_DIM**-0.5, BF16)
        k = dot(normed, weight_ref[1]).astype(BF16)
        v = (dot(normed, weight_ref[2]) + bias_ref[1:2, :].astype(F32)).astype(BF16)
        q_ref[here, :] = q
        k_ref[here, :] = k
        v_ref[here, :] = v
        q_t_ref[:, here] = q.T
        k_t_ref[:, here] = k.T
        v_t_ref[:, here] = v.T
        return carry

    lax.fori_loop(0, rows // BLOCK, project, 0)

    for start in range(0, rows, BLOCK):
        keys = start + BLOCK
        bias_t_ref[0:keys, :] = visibility(ids_col_ref, ids_row_ref, start, keys)
        for head in range(heads):
            here = slice(head * HEAD_DIM, (head + 1) * HEAD_DIM)
            q_t = keep_head(q_t_ref[:, start : start + BLOCK], head, 0)
            scores = dot(k_ref[0:keys, :], q_t) + bias_t_ref[0:keys, :]
            top = jnp.max(scores, axis=0, keepdims=True)
            weights = jnp.exp(scores - top)
            total = jnp.sum(weights, axis=0, keepdims=True)
            mixed_t = dot(v_t_ref[here, 0:keys], weights.astype(BF16)) / total
            mixed_t_ref[here, start : start + BLOCK] = mixed_t
            lse_ref[head : head + 1, start : start + BLOCK] = top + jnp.log(total)
        mixed_ref[start : start + BLOCK, :] = mixed_t_ref[:, start : start + BLOCK].T.astype(BF16)


def attend_forward(x_all, ids, gain, shift, weight, bias):
    rows, width = x_all.shape
    part = weight.shape[2]
    heads = part // HEAD_DIM
    shape = jax.ShapeDtypeStruct
    return pl.pallas_call(
        attend_forward_kernel,
        out_shape=(
            shape((rows, part), BF16),
            shape((part, rows), F32),
            shape((heads, rows), F32),
            shape((rows, width), BF16),
            shape((rows, part), BF16),
            shape((rows, part), BF16),
            shape((rows, part), BF16),
            shape((part, rows), BF16),
            shape((part, rows), BF16),
        ),
        in_specs=[whole()] * 7,
        out_specs=(whole(),) * 9,
        scratch_shapes=[pltpu.VMEM((part, rows), BF16), pltpu.VMEM((rows, BLOCK), F32)],
        compiler_params=params(),
        name="attend_forward",
    )(x_all, ids.reshape(1, rows), ids.reshape(rows, 1), gain, shift, weight, bias)


def attend_backward_kernel(
    grad_ref, q_ref, k_ref, v_ref, q_t_ref, k_t_ref, mixed_t_ref, lse_ref,
    ids_row_ref, ids_col_ref, weight_ref,
    grad_triple_ref, grad_normed_ref,
    grad_t_ref, delta_ref, grad_q_t_ref, grad_k_ref, grad_v_ref, bias_t_ref,
):
    rows, part = q_ref.shape
    heads = part // HEAD_DIM
    for start in range(0, rows, BLOCK):
        cols = slice(start, start + BLOCK)
        grad_t = grad_ref[cols, :].T
        grad_t_ref[:, cols] = grad_t
        product = grad_t.astype(F32) * mixed_t_ref[:, cols]
        for head in range(heads):
            delta_ref[head : head + 1, cols] = jnp.sum(
                product[head * HEAD_DIM : (head + 1) * HEAD_DIM, :], axis=0, keepdims=True
            )
    grad_k_ref[...] = jnp.zeros_like(grad_k_ref)
    grad_v_ref[...] = jnp.zeros_like(grad_v_ref)
    for start in range(0, rows, BLOCK):
        keys = start + BLOCK
        cols = slice(start, start + BLOCK)
        bias_t_ref[0:keys, :] = visibility(ids_col_ref, ids_row_ref, start, keys)
        for head in range(heads):
            here = slice(head * HEAD_DIM, (head + 1) * HEAD_DIM)
            scores = dot(k_ref[0:keys, :], keep_head(q_t_ref[:, cols], head, 0))
            probs = jnp.exp(scores + bias_t_ref[0:keys, :] - lse_ref[head : head + 1, cols])
            grad_probs = dot(v_ref[0:keys, :], keep_head(grad_t_ref[:, cols], head, 0))
            grad_scores = (probs * (grad_probs - delta_ref[head : head + 1, cols])).astype(BF16)
            grad_v_ref[0:keys, :] += dot(probs.astype(BF16), keep_head(grad_ref[cols, :], head, 1))
            grad_k_ref[0:keys, :] += dot(grad_scores, keep_head(q_ref[cols, :], head, 1))
            grad_q_t_ref[here, cols] = dot(k_t_ref[here, 0:keys], grad_scores)
    factor = HEAD_DIM**-0.5
    for start in range(0, rows, BLOCK):
        cols = slice(start, start + BLOCK)
        grad_q = (grad_q_t_ref[:, cols].T * factor).astype(BF16)
        grad_k = grad_k_ref[cols, :].astype(BF16)
        grad_v = grad_v_ref[cols, :].astype(BF16)
        grad_triple_ref[0, cols, :] = grad_q
        grad_triple_ref[1, cols, :] = grad_k
        grad_triple_ref[2, cols, :] = grad_v
        grad_normed_ref[cols, :] = (
            dot(grad_q, weight_ref[0], NT)
            + dot(grad_k, weight_ref[1], NT)
            + dot(grad_v, weight_ref[2], NT)
        ).astype(BF16)


def attend_backward(grad, q, k, v, q_t, k_t, mixed_t, lse, ids, weight):
    rows, part = q.shape
    heads = part // HEAD_DIM
    shape = jax.ShapeDtypeStruct
    return pl.pallas_call(
        attend_backward_kernel,
        out_shape=(shape((3, rows, part), BF16), shape((rows, weight.shape[1]), BF16)),
        in_specs=[whole()] * 11,
        out_specs=(whole(),) * 2,
        scratch_shapes=[
            pltpu.VMEM((part, rows), BF16),
            pltpu.VMEM((heads, rows), F32),
            pltpu.VMEM((part, rows), F32),
            pltpu.VMEM((rows, part), F32),
            pltpu.VMEM((rows, part), F32),
            pltpu.VMEM((rows, BLOCK), F32),
        ],
        compiler_params=params(),
        name="attend_backward",
    )(grad, q, k, v, q_t, k_t, mixed_t, lse, ids.reshape(1, rows), ids.reshape(rows, 1), weight)


def middle_kernel(
    mixed_ref, x_ref, cot_ref, ids_ref, mixer_ref, mixer_bias_ref, gain_ref, shift_ref,
    expand_ref, expand_bias_ref, reduce_ref, reduce_bias_ref, table_ref,
    out_ref, active_ref, grad_hidden_ref, normed_ref, grad_middle_ref, grad_low_ref,
    grad_mixed_ref, sums_ref,
    unit_ref, scale_ref, total_ref, grad_normed_ref,
):
    step = pl.program_id(0)
    last = pl.num_programs(0) - 1
    groups, rows, part = mixed_ref.shape
    passes = table_ref.shape[0]

    @pl.when(step == 0)
    def _():
        branch = jnp.zeros((rows, x_ref.shape[1]), F32)
        for group in range(groups):
            branch += dot(mixed_ref[group], mixer_ref[group * part : (group + 1) * part, :])
        middle = x_ref[...].astype(F32) + (branch + mixer_bias_ref[...].astype(F32))
        unit, scale = unit_rows(middle)
        normed_ref[...] = (unit * gain_ref[...].astype(F32) + shift_ref[...].astype(F32)).astype(BF16)
        unit_ref[...] = unit
        scale_ref[...] = jnp.broadcast_to(scale, scale_ref.shape)
        total_ref[...] = middle + reduce_bias_ref[...].astype(F32)
        grad_normed_ref[...] = jnp.zeros_like(grad_normed_ref)
        sums_ref[...] = jnp.zeros_like(sums_ref)

    expand = expand_ref[...]
    reduce = reduce_ref[...]
    hidden = dot(normed_ref[...], expand) + expand_bias_ref[...].astype(F32)
    square = hidden * hidden
    bend = jnp.tanh(GELU_A * hidden * (1.0 + GELU_B * square))
    half = 0.5 * (1.0 + bend)
    active = (hidden * half).astype(BF16)
    active_ref[...] = active
    total_ref[...] += dot(active, reduce)
    slope = half + (0.5 * GELU_A) * hidden * (1.0 - bend * bend) * (1.0 + (3.0 * GELU_B) * square)
    grad_hidden = (dot(cot_ref[...], reduce, NT) * slope).astype(BF16)
    grad_hidden_ref[...] = grad_hidden
    sums_ref[pl.ds(9 + step, 1), :] = jnp.sum(grad_hidden.astype(F32), axis=0, keepdims=True)
    grad_normed_ref[...] += dot(grad_hidden, expand, NT)

    @pl.when(step == last)
    def _():
        cot = cot_ref[...].astype(F32)
        embedded = jnp.zeros_like(cot)
        for index in range(passes):
            chosen = ids_ref[...] == index
            embedded += jnp.where(chosen, table_ref[index : index + 1, :].astype(F32), 0.0)
            sums_ref[index : index + 1, :] = jnp.sum(
                jnp.where(chosen, cot, 0.0), axis=0, keepdims=True
            )
        out_ref[...] = (total_ref[...] + embedded).astype(BF16)
        unit = unit_ref[...]
        grad_normed = grad_normed_ref[...]
        back = norm_pullback(grad_normed, unit, scale_ref[:, 0:1], gain_ref[...].astype(F32))
        grad_middle = cot + back
        grad_middle_ref[...] = grad_middle
        grad_low = grad_middle.astype(BF16)
        grad_low_ref[...] = grad_low
        sums_ref[5:6, :] = jnp.sum(cot, axis=0, keepdims=True)
        sums_ref[6:7, :] = jnp.sum(grad_low.astype(F32), axis=0, keepdims=True)
        sums_ref[7:8, :] = jnp.sum(grad_normed * unit, axis=0, keepdims=True)
        sums_ref[8:9, :] = jnp.sum(grad_normed, axis=0, keepdims=True)
        for group in range(groups):
            grad_mixed_ref[group] = dot(
                grad_low, mixer_ref[group * part : (group + 1) * part, :], NT
            ).astype(BF16)


def middle_part(mixed, x, cot, ids, mixer, mixer_bias, gain, shift, expand, expand_bias, reduce, reduce_bias, table):
    groups, rows, part = mixed.shape
    width, hidden = expand.shape
    chunk = width
    steps = hidden // chunk
    shape = jax.ShapeDtypeStruct

    def fixed(array):
        return pl.BlockSpec(array.shape, lambda i, n=array.ndim: (0,) * n)

    def fixed_out(dims):
        return pl.BlockSpec(dims, lambda i, n=len(dims): (0,) * n)

    return pl.pallas_call(
        middle_kernel,
        grid=(steps,),
        out_shape=(
            shape((rows, width), BF16),
            shape((rows, hidden), BF16),
            shape((rows, hidden), BF16),
            shape((rows, width), BF16),
            shape((rows, width), F32),
            shape((rows, width), BF16),
            shape((groups, rows, part), BF16),
            shape((16, width), F32),
        ),
        in_specs=[
            fixed(mixed), fixed(x), fixed(cot), fixed(ids), fixed(mixer), fixed(mixer_bias), fixed(gain), fixed(shift),
            pl.BlockSpec((width, chunk), lambda i: (0, i)),
            pl.BlockSpec((1, chunk), lambda i: (0, i)),
            pl.BlockSpec((chunk, width), lambda i: (i, 0)),
            fixed(reduce_bias), fixed(table),
        ],
        out_specs=(
            fixed_out((rows, width)),
            pl.BlockSpec((rows, chunk), lambda i: (0, i)),
            pl.BlockSpec((rows, chunk), lambda i: (0, i)),
            fixed_out((rows, width)),
            fixed_out((rows, width)),
            fixed_out((rows, width)),
            fixed_out((groups, rows, part)),
            fixed_out((16, width)),
        ),
        scratch_shapes=[
            pltpu.VMEM((rows, width), F32),
            pltpu.VMEM((rows, 128), F32),
            pltpu.VMEM((rows, width), F32),
            pltpu.VMEM((rows, width), F32),
        ],
        compiler_params=params(dimension_semantics=("arbitrary",)),
        name="middle_part",
    )(mixed, x, cot, ids, mixer, mixer_bias, gain, shift, expand, expand_bias, reduce, reduce_bias, table)


def weight_grads_kernel(mixed_ref, grad_low_ref, normed_ref, cot_ref, active_ref, grad_hidden_ref, mixer_ref, expand_ref, reduce_ref):
    step = pl.program_id(0)
    groups, rows, part = mixed_ref.shape

    @pl.when(step == 0)
    def _():
        for group in range(groups):
            mixer_ref[group * part : (group + 1) * part, :] = dot(
                mixed_ref[group], grad_low_ref[...], TN
            ).astype(BF16)

    expand_ref[...] = dot(normed_ref[...], grad_hidden_ref[...], TN).astype(BF16)
    reduce_ref[...] = dot(active_ref[...], cot_ref[...], TN).astype(BF16)


def weight_grads(mixed, grad_low, normed, cot, active, grad_hidden):
    groups, rows, part = mixed.shape
    width = normed.shape[1]
    hidden = active.shape[1]
    chunk = width
    shape = jax.ShapeDtypeStruct

    def fixed(array):
        return pl.BlockSpec(array.shape, lambda i, n=array.ndim: (0,) * n)

    return pl.pallas_call(
        weight_grads_kernel,
        grid=(hidden // chunk,),
        out_shape=(shape((width, width), BF16), shape((width, hidden), BF16), shape((hidden, width), BF16)),
        in_specs=[
            fixed(mixed), fixed(grad_low), fixed(normed), fixed(cot),
            pl.BlockSpec((rows, chunk), lambda i: (0, i)),
            pl.BlockSpec((rows, chunk), lambda i: (0, i)),
        ],
        out_specs=(
            pl.BlockSpec((width, width), lambda i: (0, 0)),
            pl.BlockSpec((width, chunk), lambda i: (0, i)),
            pl.BlockSpec((chunk, width), lambda i: (i, 0)),
        ),
        compiler_params=params(dimension_semantics=("arbitrary",)),
        name="weight_grads",
    )(mixed, grad_low, normed, cot, active, grad_hidden)


def triple_grads_kernel(x_ref, normed_ref, grad_triple_ref, grad_normed_ref, weight_ref, bias_ref, sums_ref):
    unit, _ = unit_rows(x_ref[...].astype(F32))
    grad_normed = grad_normed_ref[...].astype(F32)
    sums_ref[0:1, :] = jnp.sum(grad_normed * unit, axis=0, keepdims=True)
    sums_ref[1:2, :] = jnp.sum(grad_normed, axis=0, keepdims=True)
    for index in range(3):
        weight_ref[index] = dot(normed_ref[...], grad_triple_ref[index], TN).astype(BF16)
    bias_ref[0:1, :] = jnp.sum(grad_triple_ref[0].astype(F32), axis=0, keepdims=True)
    bias_ref[1:2, :] = jnp.sum(grad_triple_ref[2].astype(F32), axis=0, keepdims=True)


def triple_grads(x_all, normed, grad_triple, grad_normed):
    rows, width = x_all.shape
    part = grad_triple.shape[2]
    shape = jax.ShapeDtypeStruct
    return pl.pallas_call(
        triple_grads_kernel,
        out_shape=(shape((3, width, part), BF16), shape((2, part), F32), shape((2, width), F32)),
        in_specs=[whole()] * 4,
        out_specs=(whole(),) * 3,
        compiler_params=params(),
        name="triple_grads",
    )(x_all, normed, grad_triple, grad_normed)


def front_kernel(x_ref, grad_normed_ref, grad_middle_ref, gain_ref, out_ref):
    unit, scale = unit_rows(x_ref[...].astype(F32))
    back = norm_pullback(grad_normed_ref[...].astype(F32), unit, scale, gain_ref[...].astype(F32))
    out_ref[...] = (grad_middle_ref[...] + back).astype(BF16)


def front_part(x, grad_normed, grad_middle, gain):
    return pl.pallas_call(
        front_kernel,
        out_shape=jax.ShapeDtypeStruct(x.shape, BF16),
        in_specs=[whole()] * 4,
        out_specs=whole(),
        compiler_params=params(),
        name="front_part",
    )(x, grad_normed, grad_middle, gain)


def body(
    inputs,
    pass_ids,
    front_gain,
    front_shift,
    triple_weight,
    triple_bias,
    mixer_weight,
    mixer_bias,
    back_gain,
    back_shift,
    expand_weight,
    expand_bias,
    reduce_weight,
    reduce_bias,
    pass_table,
    cotangent,
):
    local_rows, width = inputs.shape
    seq_rows = pass_ids.shape[1]
    part = triple_weight.shape[2]
    groups = seq_rows // local_rows
    ids = pass_ids.reshape(seq_rows)
    own_ids = lax.dynamic_slice_in_dim(ids, lax.axis_index("narrow") * local_rows, local_rows)

    def row(vector):
        return vector.reshape(1, -1)

    x_all = lax.all_gather(inputs, "narrow", axis=0, tiled=True)
    mixed, mixed_t, lse, normed, q, k, v, q_t, k_t = attend_forward(
        x_all, ids, row(front_gain), row(front_shift), triple_weight, triple_bias
    )
    mixed_rows = lax.all_to_all(
        mixed.reshape(groups, local_rows, part), "narrow", split_axis=0, concat_axis=0, tiled=True
    )
    layer_out, active, grad_hidden, normed_two, grad_middle, grad_low, grad_mixed, sums = middle_part(
        mixed_rows, inputs, cotangent, own_ids.reshape(local_rows, 1), mixer_weight, row(mixer_bias),
        row(back_gain), row(back_shift), expand_weight, row(expand_bias), reduce_weight, row(reduce_bias), pass_table,
    )
    grad_heads = lax.all_to_all(grad_mixed, "narrow", split_axis=0, concat_axis=0, tiled=True)
    grad_mixer, grad_expand, grad_reduce = weight_grads(
        mixed_rows, grad_low, normed_two, cotangent, active, grad_hidden
    )
    grad_triple_rows, grad_normed_part = attend_backward(
        grad_heads.reshape(seq_rows, part), q, k, v, q_t, k_t, mixed_t, lse, ids, triple_weight
    )
    grad_normed = lax.psum_scatter(grad_normed_part, "narrow", scatter_dimension=0, tiled=True)
    term_weight, term_bias, front_sums = triple_grads(x_all, normed, grad_triple_rows, grad_normed_part)
    grad_inputs = front_part(inputs, grad_normed, grad_middle, row(front_gain))
    grad_triple = lax.psum(term_weight, "wide").astype(F32)

    def scatter(array):
        array = lax.psum_scatter(array, "wide", scatter_dimension=0, tiled=True)
        return lax.psum_scatter(array, "narrow", scatter_dimension=1, tiled=True).astype(F32)

    total_mixer, total_expand, total_reduce = scatter(grad_mixer), scatter(grad_expand), scatter(grad_reduce)
    grad_triple_bias = lax.psum(term_bias, "wide")
    sums, front_sums = lax.psum((sums, front_sums), ("wide", "narrow"))
    passes = pass_table.shape[0]
    return (
        layer_out,
        grad_inputs,
        front_sums[0],
        front_sums[1],
        grad_triple,
        grad_triple_bias,
        total_mixer,
        sums[6],
        sums[7],
        sums[8],
        total_expand,
        sums[9:13].reshape(-1),
        total_reduce,
        sums[5],
        sums[0:passes],
    )


def solution(mesh):
    rows = P(("wide", "narrow"), None)
    block = P("wide", "narrow")
    return jax.shard_map(
        body,
        mesh=mesh,
        in_specs=(
            rows, P("wide", None), P(), P(), P(None, None, "narrow"), P(None, "narrow"),
            P(), P(), P(), P(), P(), P(), P(), P(), P(), rows,
        ),
        out_specs=(
            rows, rows, P(), P(), P(None, None, "narrow"), P(None, "narrow"), block,
            P(), P(), P(), block, P(), block, P(), P(),
        ),
        check_vma=False,
    )
```

time: 711 us -> 451 us (0.63); the launches traced: 700 us -> 447 us
  blocking collectives: 242 us -> 69.3 us
  matrix products: 94.6 us -> 0 us
  Pallas kernels: 0 us -> 65.7 us
  other arithmetic: 38.5 us -> 2.29 us
  local copies, waits for them, and re-layouts: 48.9 us -> 27.5 us
  waiting for transfers between devices: 248 us -> 264 us
  starting transfers between devices: 12 us -> 4.02 us
    all_to_all x1, blocking collectives: 127 us -> 17.5 us  [body(): lax.all_to_all(grad_mixed, 'narrow', split_axis=0, concat_axis=0, tiled=T...]
    dot_general x26 -> x0, matrix products: 94.6 us -> none  [the longest x2 12.1 us: attend_backward(): jnp.einsum('hqk,qhe->khe', probs.astype(jnp.bfloat16), grad_block, prefer...]
    pallas_call x0 -> x6, Pallas kernels: none -> 65.7 us  [the longest x1 15.8 us: attend_forward(): pl.pallas_call(attend_forward_kernel, out_shape=(shape((rows, part), BF16...]
    all_to_all x3 -> x1, waiting for transfers between devices: 73.7 us -> 10.6 us  [body(): lax.all_to_all(mixed.reshape(groups, local_rows, part), 'narrow', split_a...]
    psum x2, blocking collectives: 106 us -> 51.8 us  [the longest x1 40 us: body(): sums, front_sums = lax.psum((sums, front_sums), ('wide', 'narrow'))]
    reduce_scatter x6 -> x5, waiting for transfers between devices: 114 us -> 168 us  [the longest x3 104 us: scatter(): array = lax.psum_scatter(array, 'wide', scatter_dimension=0, tiled=True)]
    unnamed x11, waiting for transfers between devices: 0.81 us -> 39.9 us
    all_gather x1, waiting for transfers between devices: 59.2 us -> 39.9 us  [body(): x_all = lax.all_gather(inputs, 'narrow', axis=0, tiled=True)]
  transfers between devices with their start and end apart: 12 -> 10, of which waited for: 8 -> 9; matrix products, arithmetic and copies ran while one was open for 18% -> 5% of each run, Pallas kernels for 0% -> 5%
where the time goes in v1:
time: 451 us; the launch traced here: 447 us
  waiting for transfers between devices  264 us (59%)
  blocking collectives  69.3 us (15%)
  Pallas kernels  65.7 us (15%)
  local copies, waits for them, and re-layouts  27.5 us (6%)
  between operations  14 us (3%)
    reduce_scatter x3, waiting for transfers between devices, scatter(): array = lax.psum_scatter(array, 'wide', scatter_dimension=0, tiled=True)  104 us
    reduce_scatter x1, waiting for transfers between devices, body(): lax.psum_scatter(grad_normed_part, 'narrow', scatter_dimension=0, tiled=T...  42.6 us
    psum x1, blocking collectives, body(): sums, front_sums = lax.psum((sums, front_sums), ('wide', 'narrow'))  40 us
    unnamed x11, waiting for transfers between devices  39.9 us
    all_gather x1, waiting for transfers between devices, body(): x_all = lax.all_gather(inputs, 'narrow', axis=0, tiled=True)  39.9 us
    reduce_scatter x1, waiting for transfers between devices, scatter(): lax.psum_scatter(array, 'narrow', scatter_dimension=1, tiled=True)  20.9 us
    all_to_all x1, blocking collectives, body(): lax.all_to_all(grad_mixed, 'narrow', split_axis=0, concat_axis=0, tiled=T...  17.5 us
    pallas_call x1, Pallas kernels, attend_forward(): pl.pallas_call(attend_forward_kernel, out_shape=(shape((rows, part), BF16...  15.8 us
  transfers between devices with their start and end apart: 10, of which 9 were waited for; matrix products, arithmetic and copies ran while one was open for 5% of the time, Pallas kernels for 5%

profile of v1, /device:TPU:3, one launch (start us, length us, event | category | flops | bytes accessed | tf_op | source)
XLA Modules:
  0.0 446.7 jit_solution(3711218333860311833)
XLA Ops:
  10.4 1.8 copy.42.ids_col_ref
  12.2 2.3 copy.43.weight_ref
  14.5 39.9 %all-gather.2.cloned.1.call-done.x_ref = bf16[1280,768]{1,0:T(8,128)(2,1)} async-done(((bf16[320,768]{1,0:T(8,128)(2,1)}), bf16[1280,768]{1,0:T(8,128)(2,1)}) %all-gather.2.cloned.1.call-update) | async-done | bytes 1966096 | tf_op jit(solution)/shard_map/all_gather | solution.py:443
  54.4 15.8 %attend_forward.1 = (bf16[1280,192]{1,0:T(8,128)(2,1)}, f32[192,1280]{1,0:T(8,128)}, f32[3,1280]{1,0:T(4,128)}, bf16[1280,768]{1,0:T(8,128)(2,1)}, bf16[1280,192...) custom-call(bf16[1280,768]{1,0:T(8,128)(2,1)} %all-gather.2.cloned.1, ...), custom_call_target="tpu_custom_call" | custom-call | tf_op jit(solution)/shard_map/attend_forward/pallas_call | solution.py:115
  70.3 2.2 copy.44
  72.5 3.5 all-to-all-start
  80.8 10.6 %all-to-all-done = bf16[4,320,192]{1,2,0:T(8,128)(2,1)S(1)} async-done(((bf16[4,320,192]{1,2,0:T(8,128)(2,1)}), bf16[4,320,192]{1,2,0:T(8,128)(2,1)S(1)}, u32[]{:S(2)}, u32[]{:S(2)}) %all-to-all-start) | async-done | bytes 491552 | tf_op jit(solution)/shard_map/all_to_all | solution.py:447
  92.5 15.8 %middle_part.1 = (bf16[320,768]{1,0:T(8,128)(2,1)}, bf16[320,3072]{1,0:T(8,128)(2,1)}, bf16[320,3072]{1,0:T(8,128)(2,1)}, bf16[320,768]{1,0:T(8,128)(2,1)}, f32[...) custom-call(bf16[4,320,192]{2,1,0:T(8,128)(2,1)} %copy.45.mixed_ref, ...), custom_call_target="tpu_custom_call" | custom-call | tf_op jit(solution)/shard_map/middle_part/pallas_call | solution.py:288
  108.3 9.7 %weight_grads.1 = (bf16[768,768]{1,0:T(8,128)(2,1)}, bf16[768,3072]{1,0:T(8,128)(2,1)}, bf16[3072,768]{1,0:T(8,128)(2,1)}) custom-call(bf16[4,320,192]{2,1,0:T(8,128)(2,1)} %copy.45.mixed_ref, bf16[320,768]{1,0:T(8,128)(2,1)} %get-tuple-element.57.grad_low_ref, bf16[320,768]{1,0:T(8,128)(2,1)} %get-tuple-element.58.normed_ref, bf16[320,768]{1,0:T(8,128)(2,1)} %cot_ref.3, ...), custom_call_target="tpu_custom_call" | custom-call | tf_op jit(solution)/shard_map/weight_grads/pallas_call | solution.py:354
  120.3 17.5 %all_to_all.10 = bf16[4,320,192]{1,2,0:T(8,128)(2,1)S(1)} all-to-all(bf16[4,320,192]{1,2,0:T(8,128)(2,1)S(1)} %copy.47), channel_id=1, replica_groups=mesh['wide'=8,'narrow'=4] {'narrow'}, dimensions={0} | all-to-all | bytes 983040 | tf_op jit(solution)/shard_map/all_to_all | solution.py:454
  138.9 13.9 %attend_backward.1 = (bf16[3,1280,192]{2,1,0:T(8,128)(2,1)}, bf16[1280,768]{1,0:T(8,128)(2,1)}) custom-call(bf16[1280,192]{1,0:T(8,128)(2,1)} %bitcast.9, bf16[1280,192]{1,0:T(8,128)(2,1)} %get-tuple-element.43.q_ref, bf16[1280,192]{1,0:T(8,128)(2,1)} %get-tuple-element.44.k_ref, bf16[1280,192]{1,0:T(8,128)(2,1)} %get-tuple-element.45.v_ref, ...), custom_call_target="tpu_custom_call" | custom-call | tf_op jit(solution)/shard_map/attend_backward/pallas_call | solution.py:188
  152.8 7.6 %triple_grads.1 = (bf16[3,768,192]{2,1,0:T(8,128)(2,1)}, f32[2,192]{1,0:T(2,128)}, f32[2,768]{1,0:T(2,128)}) custom-call(bf16[1280,768]{1,0:T(8,128)(2,1)} %all-gather.2.cloned.1.call-done.x_ref, bf16[1280,768]{1,0:T(8,128)(2,1)} %get-tuple-element.52.normed_ref, bf16[3,1280,192]{2,1,0:T(8,128)(2,1)} %get-tuple-element.53.grad_triple_ref, ...), custom_call_target="tpu_custom_call" | custom-call | tf_op jit(solution)/shard_map/triple_grads/pallas_call | solution.py:388
  163.1 49.4 %reduce-scatter.20.cloned.1.call-done = bf16[384,768]{1,0:T(8,128)(2,1)} async-done(((bf16[3072,768]{1,0:T(8,128)(2,1)}), bf16[384,768]{1,0:T(8,128)(2,1)}) %reduce-scatter.20.cloned.1.call-update) | async-done | bytes 589840 | tf_op jit(solution)/shard_map/reduce_scatter | solution.py:467
  212.5 2.1 copy.56
  214.7 55.0 %reduce-scatter.16.cloned.1.call-done = bf16[96,3072]{1,0:T(8,128)(2,1)} async-done(((bf16[768,3072]{1,0:T(8,128)(2,1)}), bf16[96,3072]{1,0:T(8,128)(2,1)}) %reduce-scatter.16.cloned.1.call-update) | async-done | bytes 589840 | tf_op jit(solution)/shard_map/reduce_scatter | solution.py:467
  269.8 40.0 %all-reduce = (f32[2,768]{1,0:T(2,128)S(1)}, f32[16,768]{1,0:T(8,128)S(1)}) all-reduce(f32[2,768]{1,0:T(2,128)S(1)} %copy-done.2, f32[16,768]{1,0:T(8,128)S(1)} %copy-done.1), channel_id=1, replica_groups=mesh['wide'=8,'narrow'=4] {'wide','narrow'}, use_global_device_ids=true, to_apply=%region_1.0 | all-reduce | flops 13824 | bytes 110592 | tf_op jit(solution)/shard_map/psum | solution.py:472
  311.0 11.9 %psum.30 = f32[2,192]{1,0:T(2,128)} all-reduce(f32[2,192]{1,0:T(2,128)S(1)} %copy-done.8), channel_id=1, replica_groups=mesh['wide'=8,'narrow'=4] {'wide'}, use_global_device_ids=true, to_apply=%region_3.0 | all-reduce | flops 384 | bytes 3072 | tf_op jit(solution)/shard_map/psum | solution.py:471
  323.5 5.5 %all-reduce.3.cloned.1.call-done = bf16[3,768,192]{2,1,0:T(8,128)(2,1)} async-done(((bf16[3,768,192]{2,1,0:T(8,128)(2,1)}), bf16[3,768,192]{2,1,0:T(8,128)(2,1)}) %all-reduce.3.cloned.1.call-update) | async-done | bytes 884752 | tf_op jit(solution)/shard_map/psum | solution.py:464
  329.0 2.5 copy.52
  331.5 18.4 %reduce-scatter.22.cloned.1.call-done = bf16[192,96]{1,0:T(8,128)(2,1)} async-done(((bf16[768,96]{1,0:T(8,128)(2,1)}), bf16[192,96]{1,0:T(8,128)(2,1)}) %reduce-scatter.22.cloned.1.call-update) | async-done | bytes 36880
  351.4 42.6 %reduce-scatter.12.cloned.1.call-done.grad_normed_ref = bf16[320,768]{1,0:T(8,128)(2,1)} async-done(((bf16[1280,768]{1,0:T(8,128)(2,1)}), bf16[320,768]{1,0:T(8,128)(2,1)}) %reduce-scatter.12.cloned.1.call-update) | async-done | bytes 491536 | tf_op jit(solution)/shard_map/reduce_scatter | solution.py:461
  394.0 2.9 front_part.1
  396.9 18.9 %reduce-scatter.24.cloned.1.call-done = bf16[192,384]{1,0:T(8,128)(2,1)} async-done(((bf16[768,384]{1,0:T(8,128)(2,1)}), bf16[192,384]{1,0:T(8,128)(2,1)}) %reduce-scatter.24.cloned.1.call-update) | async-done | bytes 147472
  417.7 20.9 %reduce-scatter.18.cloned.1.call-done = bf16[96,768]{1,0:T(8,128)(2,1)} async-done(((bf16[96,3072]{1,0:T(8,128)(2,1)}), bf16[96,768]{1,0:T(8,128)(2,1)}) %reduce-scatter.18.cloned.1.call-update) | async-done | bytes 147472 | tf_op jit(solution)/shard_map/reduce_scatter | solution.py:468
  (59 shorter events, 22.0 us)
Async XLA Ops:
  7.2 47.2 %all-gather.2.cloned.1.call-start = ((), (), s32[]{:S(2)}) async-start(), calls=%async_computation.9 | async-start | bytes 2457600 | tf_op jit(solution)/shard_map/all_gather | solution.py:443
  70.2 6.0 %copy-start.4 = (bf16[768]{0:T(1024)(128)(2,1)S(1)}, bf16[768]{0:T(1024)(128)(2,1)}, u32[]{:S(2)}) copy-start(bf16[768]{0:T(1024)(128)(2,1)} %param.23) | copy-start | bytes 4612
  70.2 6.6 %copy-start.5 = (bf16[768]{0:T(1024)(128)(2,1)S(1)}, bf16[768]{0:T(1024)(128)(2,1)}, u32[]{:S(2)}) copy-start(bf16[768]{0:T(1024)(128)(2,1)} %param.24) | copy-start | bytes 4612
  70.3 7.1 %copy-start.6 = (bf16[768]{0:T(1024)(128)(2,1)S(1)}, bf16[768]{0:T(1024)(128)(2,1)}, u32[]{:S(2)}) copy-start(bf16[768]{0:T(1024)(128)(2,1)} %param.25) | copy-start | bytes 4612
  70.3 7.7 %copy-start.7 = (bf16[768]{0:T(1024)(128)(2,1)S(1)}, bf16[768]{0:T(1024)(128)(2,1)}, u32[]{:S(2)}) copy-start(bf16[768]{0:T(1024)(128)(2,1)} %param.29) | copy-start | bytes 4612
  70.3 8.3 %copy-start.3 = (bf16[3072]{0:T(1024)(128)(2,1)S(1)}, bf16[3072]{0:T(1024)(128)(2,1)}, u32[]{:S(2)}) copy-start(bf16[3072]{0:T(1024)(128)(2,1)} %param.27) | copy-start | bytes 18436
  72.5 18.9 %all-to-all-start = ((bf16[4,320,192]{1,2,0:T(8,128)(2,1)}), bf16[4,320,192]{1,2,0:T(8,128)(2,1)S(1)}, u32[]{:S(2)}, u32[]{:S(2)}) async-start(bf16[4,320,192]{1,2,0:T(8,128)(2,1)} %copy.44), calls=%async_computation | async-start | bytes 1179648 | tf_op jit(solution)/shard_map/all_to_all | solution.py:447
  76.0 84.5 %reduce-scatter.14.cloned.1.call-start = ((), (), s32[]{:S(2)}) async-start(), calls=%async_computation.12 | async-start | bytes 1327104 | tf_op jit(solution)/shard_map/reduce_scatter | solution.py:467
  118.1 94.4 %reduce-scatter.20.cloned.1.call-start = ((), (), s32[]{:S(2)}) async-start(), calls=%async_computation.15 | async-start | bytes 5308416 | tf_op jit(solution)/shard_map/reduce_scatter | solution.py:467
  118.8 150.9 %reduce-scatter.16.cloned.1.call-start = ((), (), s32[]{:S(2)}) async-start(), calls=%async_computation.13 | async-start | bytes 5308416 | tf_op jit(solution)/shard_map/reduce_scatter | solution.py:467
  118.9 1.1 copy-start
  119.4 209.6 %all-reduce.3.cloned.1.call-start = ((), (), s32[]{:S(2)}) async-start(), calls=%async_computation.11 | async-start | bytes 2359296 | tf_op jit(solution)/shard_map/psum | solution.py:464
  160.4 189.5 %reduce-scatter.22.cloned.1.call-start = ((), (), s32[]{:S(2)}) async-start(), calls=%async_computation.16 | async-start | bytes 245760
  162.3 107.5 %copy-start.1 = (f32[16,768]{1,0:T(8,128)S(1)}, f32[16,768]{1,0:T(8,128)}, u32[]{:S(2)}) copy-start(f32[16,768]{1,0:T(8,128)} %get-tuple-element.62) | copy-start | bytes 147460
  162.3 107.5 %copy-start.2 = (f32[2,768]{1,0:T(2,128)S(1)}, f32[2,768]{1,0:T(2,128)}, u32[]{:S(2)}) copy-start(f32[2,768]{1,0:T(2,128)} %get-tuple-element.54) | copy-start | bytes 18436
  162.3 148.7 %copy-start.8 = (f32[2,192]{1,0:T(2,128)S(1)}, f32[2,192]{1,0:T(2,128)}, u32[]{:S(2)}) copy-start(f32[2,192]{1,0:T(2,128)} %get-tuple-element.56) | copy-start | bytes 4612
  162.3 231.7 %reduce-scatter.12.cloned.1.call-start = ((), (), s32[]{:S(2)}) async-start(), calls=%async_computation.10 | async-start | bytes 2457600 | tf_op jit(solution)/shard_map/reduce_scatter | solution.py:461
  163.0 252.7 %reduce-scatter.24.cloned.1.call-start = ((), (), s32[]{:S(2)}) async-start(), calls=%async_computation.17 | async-start | bytes 737280
  214.6 223.9 %reduce-scatter.18.cloned.1.call-start = ((), (), s32[]{:S(2)}) async-start(), calls=%async_computation.14 | async-start | bytes 737280 | tf_op jit(solution)/shard_map/reduce_scatter | solution.py:468
Sparse Core Ops, SparseCore 0:
  9.6 44.7 all-gather.1
  118.2 36.3 reduce-scatter.13
  158.5 53.9 reduce-scatter.19
  215.8 53.8 reduce-scatter.15
  273.7 55.3 all-reduce.2
  331.7 18.1 reduce-scatter.21
  352.3 41.6 reduce-scatter.11
  396.4 19.3 reduce-scatter.23
  418.2 20.3 reduce-scatter.17
